TPU v7x, 512 devices: a whole 4x4x16 slice. The times are simulated.
512 devices in a mesh: rep: 8 (over z_hi, core), fsdp: 64 (over y, z_lo, x).
Axes of the slice: x: 4, y: 4, z: 16 (z_hi: 4, z_lo: 4; z = z_hi * 4 + z_lo), core: 2. Of those that a mesh axis runs over, the one named last changes fastest.
Arguments:
- gradients: bfloat16 [8, 64, 128, 5120], P('rep', 'fsdp'), may hold values from -2 to 2
- momentum: float32 [8, 128, 5120], P('rep', 'fsdp'), may hold values from -6 to 6
Outputs:
- new_momentum: float32 [8, 128, 5120], P('rep', 'fsdp')
- update: float32 [128, 5120], P('fsdp')
All inputs are finite; a program needn't handle non-finite values.
Results may differ from a plain program's by a relative error of at most 0.0003.
Values sent between devices are 32-bit elements; how exact they have to be, the bound alone decides.
A program may use at most 64 MiB of HBM per device.

v0:
```python
import jax
import jax.numpy as jnp
from jax import lax
from jax.sharding import PartitionSpec as P

SPAN = 64
BAND = 8


decay_rate = 0.9


def cosine_basis():
    freq = jnp.arange(BAND, dtype=jnp.float32)[:, None]
    place = jnp.arange(SPAN, dtype=jnp.float32)[None, :]
    table = jnp.cos(jnp.pi * (2.0 * place + 1.0) * freq / (2.0 * SPAN)) * jnp.sqrt(2.0 / SPAN)
    return table * jnp.where(freq == 0, jnp.sqrt(0.5), 1.0)


def process(summed, moment_old, table):
    row_count = summed.shape[0]
    width = summed.shape[1]
    blended = decay_rate * moment_old + summed
    pieces = blended.reshape(row_count, width // SPAN, SPAN)
    low_band = jnp.einsum("ikj,fj->ikf", pieces, table, precision=lax.Precision.HIGHEST)
    smooth = jnp.einsum("ikf,fj->ikj", low_band, table, precision=lax.Precision.HIGHEST)
    return ((pieces - smooth).reshape(row_count, width), low_band)


def shards(gradients, momentum):
    table = cosine_basis()
    partial_grad = gradients[0, 0].astype(jnp.float32)
    moment_old = momentum[0]
    summed = lax.psum_scatter(partial_grad, "fsdp", scatter_dimension=0, tiled=True)
    fresh_moment, low_band = process(summed, moment_old, table)
    row_count = low_band.shape[0]
    block_count = low_band.shape[1]
    flat_band = low_band.reshape(row_count, block_count * BAND)
    gathered = lax.all_gather(flat_band[None], "rep", axis=0, tiled=True)
    band_total = jnp.sum(gathered, axis=0)
    band_total = band_total.reshape(row_count, block_count, BAND)
    replicas = lax.axis_size("rep")
    update = (
        jnp.einsum("ikf,fj->ikj", band_total, table, precision=lax.Precision.HIGHEST) / replicas
    )
    return (fresh_moment[None], update.reshape(row_count, block_count * SPAN))


def solution(mesh):
    return jax.shard_map(
        shards,
        mesh=mesh,
        in_specs=(P("rep", "fsdp", None, None), P("rep", "fsdp", None)),
        out_specs=(P("rep", "fsdp", None), P("fsdp", None)),
        check_vma=False,
    )
```

profile of v0, /device:TPU:1, one launch (start us, length us, event | category | flops | bytes accessed | tf_op | source)
XLA Modules:
  0.0 779.5 jit_solution(9982654071057148871)
XLA Ops:
  7.2 0.0 copy-start
  7.2 0.0 all-reduce.3.cloned.1.call-start
  7.2 3.1 bitcast_convert_fusion
  10.3 0.0 all-reduce.3.cloned.1.call-update
  10.4 1.3 dynamic-slice
  12.3 687.9 %all-reduce.3.cloned.1.call-done = f32[128,5120]{1,0:T(8,128)} async-done(((f32[128,5120]{1,0:T(8,128)}), f32[128,5120]{1,0:T(8,128)}) %all-reduce.3.cloned.1.call-update) | async-done | bytes 2621456
  700.2 0.0 copy-done
  700.2 0.9 dynamic-slice_add_fusion
  701.2 0.1 reshape.33
  701.3 0.1 copy.11
  701.4 0.2 fusion.2
  701.6 0.2 copy.13
  701.8 0.3 convolution_subtract_fusion
  702.1 0.1 copy.12
  702.2 0.7 broadcast_in_dim_reshape.6
  702.9 0.1 broadcast_in_dim_reshape.7
  703.0 68.2 %all_gather.3 = f32[8,2,640]{2,1,0:T(2,128)S(1)} all-gather(f32[1,2,640]{2,1,0:T(2,128)S(1)} %broadcast_in_dim_reshape.7), channel_id=1, replica_groups=mesh['rep'=8,'fsdp'=64] {'rep'}, dimensions={0}, use_global_device_ids=true | all-gather | bytes 46080 | tf_op jit(solution)/shard_map/all_gather | solution.py:39
  771.3 0.1 reshape.34
  771.4 0.4 convolution_multiply_fusion
  771.8 0.1 copy.15
  771.9 0.7 reshape.35
  (3 shorter events, 0.0 us)
Async XLA Ops:
  7.2 693.1 %copy-start = (f32[1,2,5120]{2,1,0:T(2,128)S(1)}, f32[1,2,5120]{2,1,0:T(2,128)}, u32[]{:S(2)}) copy-start(f32[1,2,5120]{2,1,0:T(2,128)} %param.3) | copy-start | bytes 122884
  7.2 693.1 %all-reduce.3.cloned.1.call-start = ((), (), s32[]{:S(2)}) async-start(), calls=%async_computation | async-start | bytes 5242880
Sparse Core Ops, SparseCore 0:
  10.9 689.2 all-reduce.2
where the time goes:
time: 780 us; the launch traced here: 779 us
  waiting for transfers between devices  688 us (88%)
  blocking collectives  68.2 us (9%)
  between operations  14.7 us (2%)
    unnamed x2, waiting for transfers between devices  688 us
    all_gather x1, blocking collectives, shards(): gathered = lax.all_gather(flat_band[None], 'rep', axis=0, tiled=True)  68.2 us
  transfers between devices with their start and end apart: 1, of which 1 were waited for; matrix products, arithmetic and copies ran while one was open for 0% of the time, Pallas kernels for 0%

commit v1 on v0

v1 whole, which is shorter than its diff:
```python
import jax
import jax.numpy as jnp
import ml_dtypes
import numpy as np
from jax import lax
from jax.experimental import pallas as pl
from jax.experimental.pallas import tpu as pltpu
from jax.sharding import PartitionSpec as P

SPAN = 64
BAND = 8
D = 5120
ROWS = 128
GROUP = 1024
GROUPS = D // GROUP
DECAY = 0.9
MESH = pl.DeviceIdType.MESH

CHUNKS = (
    ("zxy", 0, 1024),
    ("xyz", 1024, 1024),
    ("yxz", 2048, 1024),
    ("xyz", 3072, 1024),
    ("yxz", 4096, 1024),
)
N_CHUNKS = len(CHUNKS)
REPS = 8


def halves():
    freq = np.arange(BAND)[:, None]
    place = np.arange(SPAN)[None, :]
    table = np.cos(np.pi * (2.0 * place + 1.0) * freq / (2.0 * SPAN)) * np.sqrt(2.0 / SPAN)
    table = table * np.where(freq == 0, np.sqrt(0.5), 1.0)
    full = np.zeros((GROUP, GROUP // SPAN * BAND), np.float32)
    for block in range(GROUP // SPAN):
        full[block * SPAN : (block + 1) * SPAN, block * BAND : (block + 1) * BAND] = table.T
    high = full.astype(ml_dtypes.bfloat16)
    low = (full - high.astype(np.float32)).astype(ml_dtypes.bfloat16)
    return np.concatenate([high, low], axis=1)


def permutation(order):
    weight = {"y": 32, "z": 8, "x": 2}
    row = lax.broadcasted_iota(jnp.int32, (ROWS, ROWS), 0)
    column = lax.broadcasted_iota(jnp.int32, (ROWS, ROWS), 1)
    source = (
        ((row >> 5) & 3) * weight[order[0]]
        + ((row >> 3) & 3) * weight[order[1]]
        + ((row >> 1) & 3) * weight[order[2]]
        + (row & 1)
    )
    return jnp.where(source == column, 1.0, 0.0).astype(jnp.bfloat16)


def split(value):
    high = value.astype(jnp.bfloat16)
    return high, (value - high.astype(jnp.float32)).astype(jnp.bfloat16)


def analyse(value, basis_high, basis_low):
    high, low = split(value)
    dims = (((1,), (0,)), ((), ()))
    f32 = jnp.float32
    return (
        lax.dot_general(high, basis_high, dims, preferred_element_type=f32)
        + lax.dot_general(high, basis_low, dims, preferred_element_type=f32)
        + lax.dot_general(low, basis_high, dims, preferred_element_type=f32)
    )


def expand(value, basis_high, basis_low):
    high, low = split(value)
    dims = (((1,), (1,)), ((), ()))
    f32 = jnp.float32
    return (
        lax.dot_general(high, basis_high, dims, preferred_element_type=f32)
        + lax.dot_general(high, basis_low, dims, preferred_element_type=f32)
        + lax.dot_general(low, basis_high, dims, preferred_element_type=f32)
    )


def kernel(g_hbm, m_hbm, b_hbm, fresh_ref, update_ref, *scratch):
    scratch = list(scratch)
    g_ref, m_ref, b_ref, stack, bands = scratch[:5]
    per = scratch[5 : 5 + 6 * N_CHUNKS]
    load_sems, send_sems, recv_sems, rep_send, rep_recv = scratch[5 + 6 * N_CHUNKS :]

    rep = lax.axis_index("rep")
    fsdp = lax.axis_index("fsdp")
    at = {"y": fsdp // 16, "z": (fsdp // 4) % 4, "x": fsdp % 4}
    stride = {"y": 16, "z": 4, "x": 1}

    def peer(axis, k):
        there = lax.rem(at[axis] + k, 4)
        return there, {"rep": rep, "fsdp": fsdp + (there - at[axis]) * stride[axis]}

    def rep_peer(k):
        return {"rep": lax.rem(rep + k, REPS), "fsdp": fsdp}

    barrier = pltpu.get_barrier_semaphore()
    for k in range(1, REPS):
        pl.semaphore_signal(barrier, inc=1, device_id=rep_peer(k), device_id_type=MESH)
    for axis in "xyz":
        for k in range(1, 4):
            pl.semaphore_signal(barrier, inc=1, device_id=peer(axis, k)[1], device_id_type=MESH)

    loads = []
    for c, (order, first, width) in enumerate(CHUNKS):
        columns = pl.ds(first, width)
        loads.append(
            pltpu.make_async_copy(g_hbm.at[0, 0, :, columns], g_ref.at[:, columns], load_sems.at[c])
        )
        loads[-1].start()
    m_load = pltpu.make_async_copy(m_hbm.at[0], m_ref, load_sems.at[N_CHUNKS])
    b_load = pltpu.make_async_copy(b_hbm, b_ref, load_sems.at[N_CHUNKS + 1])
    m_load.start()
    b_load.start()

    turned = {order: permutation(order) for order in sorted({c[0] for c in CHUNKS})}
    stack[...] = jnp.zeros_like(stack)

    def copies(c, phase):
        order = CHUNKS[c][0]
        t_ref, s_ref, u_ref, r1, r2, r3 = per[6 * c : 6 * c + 6]
        result = []
        for k in range(1, 4):
            there, device = peer(order[phase], k)
            if phase == 0:
                source, target = t_ref.at[pl.ds(pl.multiple_of(there * 32, 32), 32)], r1.at[k - 1]
            elif phase == 1:
                source, target = s_ref.at[pl.ds(pl.multiple_of(there * 8, 8), 8)], r2.at[k - 1]
            else:
                source, target = u_ref.at[there], r3.at[k - 1]
            index = (c * 3 + phase) * 3 + k - 1
            result.append(
                pltpu.make_async_remote_copy(
                    src_ref=source,
                    dst_ref=target,
                    send_sem=send_sems.at[index],
                    recv_sem=recv_sems.at[index],
                    device_id=device,
                    device_id_type=MESH,
                )
            )
        return result

    def turn(c):
        order, first, width = CHUNKS[c]
        loads[c].wait()
        per[6 * c][...] = jnp.dot(
            turned[order], g_ref[:, first : first + width], preferred_element_type=jnp.float32
        )

    def go(c, phase):
        for copy in copies(c, phase):
            copy.start()

    turn(0)
    pl.semaphore_wait(barrier, REPS - 1 + 9)
    go(0, 0)
    for c in range(1, N_CHUNKS):
        turn(c)
        go(c, 0)

    def second(c):
        order, first, width = CHUNKS[c]
        t_ref, s_ref, u_ref, r1, r2, r3 = per[6 * c : 6 * c + 6]
        for copy in copies(c, 0):
            copy.wait_recv()
        own = pl.ds(pl.multiple_of(at[order[0]] * 32, 32), 32)
        s_ref[...] = (t_ref[own, :] + r1[0]) + (r1[1] + r1[2])
        go(c, 1)

    def third(c):
        order, first, width = CHUNKS[c]
        t_ref, s_ref, u_ref, r1, r2, r3 = per[6 * c : 6 * c + 6]
        for copy in copies(c, 1):
            copy.wait_recv()
        own = pl.ds(pl.multiple_of(at[order[1]] * 8, 8), 8)
        total = (s_ref[own, :] + r2[0]) + (r2[1] + r2[2])
        for q in range(4):
            u_ref[q] = total[2 * q : 2 * q + 2]
        go(c, 2)

    def last(c):
        order, first, width = CHUNKS[c]
        t_ref, s_ref, u_ref, r1, r2, r3 = per[6 * c : 6 * c + 6]
        for copy in copies(c, 2):
            copy.wait_recv()
        total = (u_ref[at[order[2]]] + r3[0]) + (r3[1] + r3[2])
        columns = slice(first, first + width)
        blended = DECAY * m_ref[:, columns] + total
        for part in range(width // GROUP):
            g = first // GROUP + part
            stack[2 * g : 2 * g + 2, :] = blended[:, part * GROUP : (part + 1) * GROUP]

    m_load.wait()
    b_load.wait()
    for step in range(N_CHUNKS + 2):
        if step < N_CHUNKS:
            second(step)
        if 0 <= step - 1 < N_CHUNKS:
            third(step - 1)
        if 0 <= step - 2 < N_CHUNKS:
            last(step - 2)

    high, low = b_ref[:, :128], b_ref[:, 128:]
    blended = stack[...]
    band = analyse(blended, high, low)
    bands[0] = band
    shares = []
    for k in range(1, REPS):
        copy = pltpu.make_async_remote_copy(
            src_ref=bands.at[0],
            dst_ref=bands.at[k],
            send_sem=rep_send.at[k - 1],
            recv_sem=rep_recv.at[k - 1],
            device_id=rep_peer(k),
            device_id_type=MESH,
        )
        copy.start()
        shares.append(copy)
    fresh = blended - expand(band, high, low)
    for g in range(GROUPS):
        fresh_ref[0, :, g * GROUP : (g + 1) * GROUP] = fresh[2 * g : 2 * g + 2]
    for copy in shares:
        copy.wait_recv()
    total = band
    for k in range(1, REPS):
        total = total + bands[k]
    update = expand(total * (1.0 / REPS), high, low)
    for g in range(GROUPS):
        update_ref[:, g * GROUP : (g + 1) * GROUP] = update[2 * g : 2 * g + 2]
    for c in range(N_CHUNKS):
        for phase in range(3):
            for copy in copies(c, phase):
                copy.wait_send()
    for copy in shares:
        copy.wait_send()


def shards(gradients, momentum):
    basis = jnp.asarray(halves())
    f32 = jnp.float32
    per = []
    for order, first, width in CHUNKS:
        per += [
            pltpu.VMEM((ROWS, width), f32),
            pltpu.VMEM((32, width), f32),
            pltpu.VMEM((4, 2, width), f32),
            pltpu.VMEM((3, 32, width), f32),
            pltpu.VMEM((3, 8, width), f32),
            pltpu.VMEM((3, 2, width), f32),
        ]
    return pl.pallas_call(
        kernel,
        out_shape=(
            jax.ShapeDtypeStruct((1, 2, D), f32),
            jax.ShapeDtypeStruct((2, D), f32),
        ),
        in_specs=[pl.BlockSpec(memory_space=pl.ANY)] * 3,
        out_specs=(pl.BlockSpec(memory_space=pltpu.VMEM),) * 2,
        scratch_shapes=[
            pltpu.VMEM((ROWS, D), jnp.bfloat16),
            pltpu.VMEM((2, D), f32),
            pltpu.VMEM((GROUP, 256), jnp.bfloat16),
            pltpu.VMEM((16, GROUP), f32),
            pltpu.VMEM((REPS, 16, 128), f32),
            *per,
            pltpu.SemaphoreType.DMA((N_CHUNKS + 2,)),
            pltpu.SemaphoreType.DMA((9 * N_CHUNKS,)),
            pltpu.SemaphoreType.DMA((9 * N_CHUNKS,)),
            pltpu.SemaphoreType.DMA((REPS - 1,)),
            pltpu.SemaphoreType.DMA((REPS - 1,)),
        ],
        compiler_params=pltpu.CompilerParams(
            collective_id=0, has_side_effects=True, vmem_limit_bytes=48 << 20
        ),
        name="momentum_step",
    )(gradients, momentum, basis)


def solution(mesh):
    return jax.shard_map(
        shards,
        mesh=mesh,
        in_specs=(P("rep", "fsdp", None, None), P("rep", "fsdp", None)),
        out_specs=(P("rep", "fsdp", None), P("fsdp", None)),
        check_vma=False,
    )
```

time: 780 us -> 58.5 us (0.07)
  waiting for transfers between devices: 688 us -> 0 us
  blocking collectives: 68.2 us -> 0 us
  Pallas kernels: 0 us -> 53.3 us
  between operations: 14.7 us -> 0.65 us
    unnamed x2 -> x0, waiting for transfers between devices: 688 us -> none
    all_gather x1 -> x0, blocking collectives: 68.2 us -> none  [shards(): gathered = lax.all_gather(flat_band[None], 'rep', axis=0, tiled=True)]
    pallas_call x0 -> x1, Pallas kernels: none -> 53.3 us  [shards(): pl.pallas_call(kernel, out_shape=(jax.ShapeDtypeStruct((1, 2, D), f32), j...]
  transfers between devices with their start and end apart: 1 -> 0, of which waited for: 1 -> 0; matrix products, arithmetic and copies ran while one was open for 0% -> 0% of each run, Pallas kernels for 0% -> 0%
where the time goes in v1:
time: 58.5 us; the launch traced here: 58.3 us
  Pallas kernels  53.3 us (91%)
  local copies, waits for them, and re-layouts  4.37 us (7%)
  between operations  0.65 us (1%)
    pallas_call x1, Pallas kernels, shards(): pl.pallas_call(kernel, out_shape=(jax.ShapeDtypeStruct((1, 2, D), f32), j...  53.3 us
    unnamed x8, local copies, waits for them, and re-layouts  4.37 us

profile of v1, /device:TPU:1, one launch (start us, length us, event | category | flops | bytes accessed | tf_op | source)
XLA Modules:
  0.0 58.3 jit_solution(14954741397768024379)
XLA Ops:
  0.6 0.0 copy-start
  0.6 1.3 %copy-done = bf16[1,1,128,5120]{3,2,1,0:T(8,128)(2,1)S(1)} copy-done((bf16[1,1,128,5120]{3,2,1,0:T(8,128)(2,1)S(1)}, bf16[1,1,128,5120]{3,2,1,0:T(8,128)(2,1)}, u32[]{:S(2)}) %copy-start) | copy-done | bytes 1310744
  1.9 0.0 copy-start.1
  1.9 1.0 %copy-done.1 = bf16[1024,256]{1,0:T(8,128)(2,1)S(1)} copy-done((bf16[1024,256]{1,0:T(8,128)(2,1)S(1)}, bf16[1024,256]{1,0:T(8,128)(2,1)}, u32[]{:S(2)}) %copy-start.1) | copy-done | bytes 524312
  3.0 0.0 copy-start.2
  3.0 0.8 %copy-done.2 = f32[1,2,5120]{2,1,0:T(2,128)S(1)} copy-done((f32[1,2,5120]{2,1,0:T(2,128)S(1)}, f32[1,2,5120]{2,1,0:T(2,128)}, u32[]{:S(2)}) %copy-start.2) | copy-done | bytes 40984
  3.8 53.3 %momentum_step.1 = (f32[1,2,5120]{2,1,0:T(2,128)S(1)}, f32[2,5120]{1,0:T(2,128)S(1)}) custom-call(bf16[1,1,128,5120]{3,2,1,0:T(8,128)(2,1)S(1)} %copy-done, f32[1,2,5120]{2,1,0:T(2,128)S(1)} %copy-done.2, bf16[1024,256]{1,0:T(8,128)(2,1)S(1)} %copy-done.1), custom_call_target="tpu_custom_call" | custom-call | tf_op jit(solution)/shard_map/momentum_step/pallas_call | solution.py:256
  57.0 0.6 %copy.7 = f32[1,2,5120]{2,1,0:T(2,128)} copy(f32[1,2,5120]{2,1,0:T(2,128)S(1)} %get-tuple-element.4) | data formatting | bytes 81920
  57.7 0.6 %copy.8 = f32[2,5120]{1,0:T(2,128)} copy(f32[2,5120]{1,0:T(2,128)S(1)} %get-tuple-element.5) | data formatting | bytes 81920
Async XLA Ops:
  0.6 1.3 %copy-start = (bf16[1,1,128,5120]{3,2,1,0:T(8,128)(2,1)S(1)}, bf16[1,1,128,5120]{3,2,1,0:T(8,128)(2,1)}, u32[]{:S(2)}) copy-start(bf16[1,1,128,5120]{3,2,1,0:T(8,128)(2,1)} %g_hbm.1) | copy-start | bytes 3932164
  1.9 1.0 %copy-start.1 = (bf16[1024,256]{1,0:T(8,128)(2,1)S(1)}, bf16[1024,256]{1,0:T(8,128)(2,1)}, u32[]{:S(2)}) copy-start(bf16[1024,256]{1,0:T(8,128)(2,1)} %constant.2.clone.b_hbm) | copy-start | bytes 1572868
  3.0 0.8 %copy-start.2 = (f32[1,2,5120]{2,1,0:T(2,128)S(1)}, f32[1,2,5120]{2,1,0:T(2,128)}, u32[]{:S(2)}) copy-start(f32[1,2,5120]{2,1,0:T(2,128)} %m_hbm.1) | copy-start | bytes 122884

commit v2 on v1

v2 whole, which is shorter than its diff:
```python
import jax
import jax.numpy as jnp
import ml_dtypes
import numpy as np
from jax import lax
from jax.experimental import pallas as pl
from jax.experimental.pallas import tpu as pltpu
from jax.sharding import PartitionSpec as P

SPAN = 64
BAND = 8
D = 5120
ROWS = 128
GROUP = 1024
GROUPS = D // GROUP
DECAY = 0.9
MESH = pl.DeviceIdType.MESH

REPS = 8
RING = 16

CHUNKS = (
    ("xyz", 0, 512),
    ("yxz", 512, 512),
    ("zxy", 1024, 512),
    ("xyz", 1536, 896),
    ("yxz", 2432, 896),
    ("xyz", 3328, 896),
    ("yxz", 4224, 896),
)
N_CHUNKS = len(CHUNKS)
SETS = (("xyz", 0, 2), ("yxz", 2, 3))
BANDS = D // SPAN * BAND


def halves():
    freq = np.arange(BAND)[:, None]
    place = np.arange(SPAN)[None, :]
    table = np.cos(np.pi * (2.0 * place + 1.0) * freq / (2.0 * SPAN)) * np.sqrt(2.0 / SPAN)
    table = table * np.where(freq == 0, np.sqrt(0.5), 1.0)
    full = np.zeros((GROUP, GROUP // SPAN * BAND), np.float32)
    for block in range(GROUP // SPAN):
        full[block * SPAN : (block + 1) * SPAN, block * BAND : (block + 1) * BAND] = table.T
    high = full.astype(ml_dtypes.bfloat16)
    low = (full - high.astype(np.float32)).astype(ml_dtypes.bfloat16)
    return np.concatenate([high, low], axis=1)


def permutation(order):
    weight = {"y": 32, "z": 8, "x": 2}
    row = lax.broadcasted_iota(jnp.int32, (ROWS, ROWS), 0)
    column = lax.broadcasted_iota(jnp.int32, (ROWS, ROWS), 1)
    source = (
        ((row >> 5) & 3) * weight[order[0]]
        + ((row >> 3) & 3) * weight[order[1]]
        + ((row >> 1) & 3) * weight[order[2]]
        + (row & 1)
    )
    return jnp.where(source == column, 1.0, 0.0).astype(jnp.bfloat16)


def split(value):
    high = value.astype(jnp.bfloat16)
    return high, (value - high.astype(jnp.float32)).astype(jnp.bfloat16)


def analyse(value, basis_high, basis_low):
    high, low = split(value)
    dims = (((1,), (0,)), ((), ()))
    f32 = jnp.float32
    return (
        lax.dot_general(high, basis_high, dims, preferred_element_type=f32)
        + lax.dot_general(high, basis_low, dims, preferred_element_type=f32)
        + lax.dot_general(low, basis_high, dims, preferred_element_type=f32)
    )


def expand(value, basis_high, basis_low):
    high, low = split(value)
    dims = (((1,), (1,)), ((), ()))
    f32 = jnp.float32
    return (
        lax.dot_general(high, basis_high, dims, preferred_element_type=f32)
        + lax.dot_general(high, basis_low, dims, preferred_element_type=f32)
        + lax.dot_general(low, basis_high, dims, preferred_element_type=f32)
    )


def kernel(g_hbm, m_hbm, b_hbm, fresh_ref, update_ref, *scratch):
    scratch = list(scratch)
    take = lambda n: [scratch.pop(0) for _ in range(n)]
    g_ref, m_ref, b_ref, stack, band_stack = take(5)
    per = take(6 * N_CHUNKS)
    low_per = take(4 * len(SETS))
    ring_out, ring_in, pair_out, pair_in, old_ref = take(5)
    load_sems, send_sems, recv_sems, low_send, low_recv = take(5)
    ring_send, ring_recv, pair_send, pair_recv, relay = take(5)

    rep = lax.axis_index("rep")
    fsdp = lax.axis_index("fsdp")
    core = rep % 2
    at = {"y": fsdp // 16, "z": (fsdp // 4) % 4, "x": fsdp % 4}
    stride = {"y": 16, "z": 4, "x": 1}
    height = (rep // 2) * 4 + at["z"]

    def peer(axis, k):
        there = lax.rem(at[axis] + k, 4)
        return there, {"rep": rep, "fsdp": fsdp + (there - at[axis]) * stride[axis]}

    def ring_peer(k):
        there = lax.rem(height + k, RING)
        low = there % 4
        return low, {"rep": (there // 4) * 2 + core, "fsdp": fsdp + (low - at["z"]) * 4}

    other = {"rep": rep + 1 - 2 * core, "fsdp": fsdp}

    barrier = pltpu.get_barrier_semaphore()
    greeted = [ring_peer(k)[1] for k in (3, 13, 2, 14, 1, 15)]
    greeted += [peer(axis, k)[1] for k in (2, 1, 3) for axis in "xy"]
    greeted.append(other)
    for device in greeted:
        pl.semaphore_signal(barrier, inc=1, device_id=device, device_id_type=MESH)

    loads = []
    for g in range(GROUPS):
        columns = pl.ds(g * GROUP, GROUP)
        loads.append(
            pltpu.make_async_copy(g_hbm.at[0, 0, :, columns], g_ref.at[:, columns], load_sems.at[g])
        )
    b_load = pltpu.make_async_copy(b_hbm, b_ref, load_sems.at[GROUPS + 1])
    m_load = pltpu.make_async_copy(m_hbm.at[0], m_ref, load_sems.at[GROUPS])
    b_load.start()
    for load in loads:
        load.start()
    m_load.start()

    turned = {order: permutation(order) for order in ("xyz", "yxz", "zxy")}
    stack[...] = jnp.zeros_like(stack)
    band_stack[...] = jnp.zeros_like(band_stack)

    def remote(source, target, sends, recvs, index, device):
        return pltpu.make_async_remote_copy(
            src_ref=source,
            dst_ref=target,
            send_sem=sends.at[index],
            recv_sem=recvs.at[index],
            device_id=device,
            device_id_type=MESH,
        )

    def copies(c, phase):
        order = CHUNKS[c][0]
        t_ref, s_ref, u_ref, r1, r2, r3 = per[6 * c : 6 * c + 6]
        result = []
        for k in (2, 1, 3):
            there, device = peer(order[phase], k)
            if phase == 0:
                source, target = t_ref.at[pl.ds(pl.multiple_of(there * 32, 32), 32)], r1.at[k - 1]
            elif phase == 1:
                source, target = s_ref.at[pl.ds(pl.multiple_of(there * 8, 8), 8)], r2.at[k - 1]
            else:
                source, target = u_ref.at[there], r3.at[k - 1]
            index = (c * 3 + phase) * 3 + k - 1
            result.append(remote(source, target, send_sems, recv_sems, index, device))
        return result

    def low_copies(n, phase):
        order = SETS[n][0]
        l_ref, s_ref, r1, r2 = low_per[4 * n : 4 * n + 4]
        result = []
        for k in (2, 1, 3):
            there, device = peer(order[phase], k)
            if phase == 0:
                source, target = l_ref.at[pl.ds(pl.multiple_of(there * 32, 32), 32)], r1.at[k - 1]
            else:
                source, target = s_ref.at[pl.ds(pl.multiple_of(there * 8, 8), 8)], r2.at[k - 1]
            index = (n * 2 + phase) * 3 + k - 1
            result.append(remote(source, target, low_send, low_recv, index, device))
        return result

    def ring_copies():
        result = []
        for k in (8, 7, 9, 6, 10, 5, 11, 4, 12, 3, 13, 2, 14, 1, 15):
            low, device = ring_peer(k)
            result.append(
                remote(ring_out.at[low], ring_in.at[k - 1], ring_send, ring_recv, k - 1, device)
            )
        return result

    def pair_copy():
        return remote(pair_out, pair_in, pair_send, pair_recv, 0, other)

    def start(batch):
        for copy in batch:
            copy.start()

    def arrive(batch):
        for copy in batch:
            copy.wait_recv()

    def turn(c):
        order, first, width = CHUNKS[c]
        per[6 * c][...] = jnp.dot(
            turned[order], g_ref[:, first : first + width], preferred_element_type=jnp.float32
        )

    def low_first(n):
        order, first, count = SETS[n]
        for j in range(count):
            begin = (first + j) * GROUP
            loads[first + j].wait()
            both = jnp.dot(
                g_ref[:, begin : begin + GROUP], b_ref[...], preferred_element_type=jnp.float32
            )
            high, low = split(both[:, :128] + both[:, 128:])
            low_per[4 * n][:, j * 128 : (j + 1) * 128] = jnp.dot(
                turned[order], high, preferred_element_type=jnp.float32
            ) + jnp.dot(turned[order], low, preferred_element_type=jnp.float32)

    def low_second(n):
        l_ref, s_ref, r1, r2 = low_per[4 * n : 4 * n + 4]
        arrive(low_copies(n, 0))
        own = pl.ds(pl.multiple_of(at[SETS[n][0][0]] * 32, 32), 32)
        s_ref[...] = (l_ref[own, :] + r1[0]) + (r1[1] + r1[2])
        start(low_copies(n, 1))

    def low_third(n):
        l_ref, s_ref, r1, r2 = low_per[4 * n : 4 * n + 4]
        order, first, count = SETS[n]
        arrive(low_copies(n, 1))
        own = pl.ds(pl.multiple_of(at[order[1]] * 8, 8), 8)
        total = (s_ref[own, :] + r2[0]) + (r2[1] + r2[2])
        for q in range(4):
            ring_out[q, :, first * 128 : (first + count) * 128] = total[2 * q : 2 * q + 2]

    def second(c):
        order, first, width = CHUNKS[c]
        t_ref, s_ref, u_ref, r1, r2, r3 = per[6 * c : 6 * c + 6]
        arrive(copies(c, 0))
        own = pl.ds(pl.multiple_of(at[order[0]] * 32, 32), 32)
        s_ref[...] = (t_ref[own, :] + r1[0]) + (r1[1] + r1[2])
        start(copies(c, 1))

    def third(c):
        order, first, width = CHUNKS[c]
        t_ref, s_ref, u_ref, r1, r2, r3 = per[6 * c : 6 * c + 6]
        arrive(copies(c, 1))
        own = pl.ds(pl.multiple_of(at[order[1]] * 8, 8), 8)
        total = (s_ref[own, :] + r2[0]) + (r2[1] + r2[2])
        for q in range(4):
            u_ref[q] = total[2 * q : 2 * q + 2]
        start(copies(c, 2))

    def last(c):
        order, first, width = CHUNKS[c]
        t_ref, s_ref, u_ref, r1, r2, r3 = per[6 * c : 6 * c + 6]
        arrive(copies(c, 2))
        total = (u_ref[at[order[2]]] + r3[0]) + (r3[1] + r3[2])
        blended = DECAY * m_ref[:, first : first + width] + total
        begin = first
        while begin < first + width:
            g = begin // GROUP
            end = min(first + width, (g + 1) * GROUP)
            stack[2 * g : 2 * g + 2, begin - g * GROUP : end - g * GROUP] = blended[
                :, begin - first : end - first
            ]
            begin = end

    def low_fourth():
        arrive(ring_copies())
        terms = [ring_out[at["z"]]] + [ring_in[k] for k in range(RING - 1)]
        while len(terms) > 1:
            terms = [terms[j] + terms[j + 1] for j in range(0, len(terms), 2)]
        pair_out[...] = terms[0]
        pair_copy().start()

    def relay_signal(j):
        for k in (3, 13):
            pl.semaphore_signal(
                relay.at[j], inc=1, device_id=ring_peer(k)[1], device_id_type=MESH
            )

    b_load.wait()
    for n in range(len(SETS)):
        low_first(n)
    for c in range(3):
        turn(c)
    pl.semaphore_wait(barrier, len(greeted))
    relay_signal(0)
    for n in range(len(SETS)):
        start(low_copies(n, 0))
    for c in range(3):
        start(copies(c, 0))
    m_load.wait()
    high, low = b_ref[:, :128], b_ref[:, 128:]
    old = DECAY * m_ref[...]
    for g in range(GROUPS):
        stack[2 * g : 2 * g + 2, :] = old[:, g * GROUP : (g + 1) * GROUP]
    old_band = analyse(stack[...], high, low)
    for g in range(GROUPS):
        old_ref[:, g * 128 : (g + 1) * 128] = old_band[2 * g : 2 * g + 2]
    for c in range(3, N_CHUNKS):
        turn(c)
    for n in range(len(SETS)):
        low_second(n)
    for c in (3, 4):
        start(copies(c, 0))
    pl.semaphore_wait(relay.at[0], 2)
    relay_signal(1)
    second(0)
    second(1)
    for c in (5, 6):
        start(copies(c, 0))
    for n in range(len(SETS)):
        low_third(n)
    ring_out[at["z"]] = ring_out[at["z"]] + old_ref[...]
    pl.semaphore_wait(relay.at[1], 2)
    start(ring_copies())
    second(2)
    second(3)
    second(4)
    third(0)
    third(1)
    third(2)
    second(5)
    second(6)
    third(3)
    third(4)
    last(0)
    last(1)
    last(2)
    third(5)
    third(6)
    low_fourth()
    last(3)
    last(4)
    arrive([pair_copy()])
    for g in range(GROUPS):
        lanes = slice(g * 128, (g + 1) * 128)
        band_stack[2 * g : 2 * g + 2, :] = pair_out[:, lanes] + pair_in[:, lanes]
    update = expand(band_stack[...] * (1.0 / REPS), high, low)
    for g in range(GROUPS):
        update_ref[:, g * GROUP : (g + 1) * GROUP] = update[2 * g : 2 * g + 2]
    last(5)
    last(6)
    blended = stack[...]
    fresh = blended - expand(analyse(blended, high, low), high, low)
    for g in range(GROUPS):
        fresh_ref[0, :, g * GROUP : (g + 1) * GROUP] = fresh[2 * g : 2 * g + 2]
    sent = [copy for c in range(N_CHUNKS) for phase in range(3) for copy in copies(c, phase)]
    sent += [copy for n in range(len(SETS)) for phase in range(2) for copy in low_copies(n, phase)]
    sent += ring_copies() + [pair_copy()]
    for copy in sent:
        copy.wait_send()


def shards(gradients, momentum):
    basis = jnp.asarray(halves())
    f32 = jnp.float32
    per = []
    for order, first, width in CHUNKS:
        per += [
            pltpu.VMEM((ROWS, width), f32),
            pltpu.VMEM((32, width), f32),
            pltpu.VMEM((4, 2, width), f32),
            pltpu.VMEM((3, 32, width), f32),
            pltpu.VMEM((3, 8, width), f32),
            pltpu.VMEM((3, 2, width), f32),
        ]
    low_per = []
    for order, first, count in SETS:
        width = count * 128
        low_per += [
            pltpu.VMEM((ROWS, width), f32),
            pltpu.VMEM((32, width), f32),
            pltpu.VMEM((3, 32, width), f32),
            pltpu.VMEM((3, 8, width), f32),
        ]
    return pl.pallas_call(
        kernel,
        out_shape=(
            jax.ShapeDtypeStruct((1, 2, D), f32),
            jax.ShapeDtypeStruct((2, D), f32),
        ),
        in_specs=[pl.BlockSpec(memory_space=pltpu.HBM)] * 3,
        out_specs=(pl.BlockSpec(memory_space=pltpu.VMEM),) * 2,
        scratch_shapes=[
            pltpu.VMEM((ROWS, D), jnp.bfloat16),
            pltpu.VMEM((2, D), f32),
            pltpu.VMEM((GROUP, 256), jnp.bfloat16),
            pltpu.VMEM((16, GROUP), f32),
            pltpu.VMEM((16, 128), f32),
            *per,
            *low_per,
            pltpu.VMEM((4, 2, BANDS), f32),
            pltpu.VMEM((RING - 1, 2, BANDS), f32),
            pltpu.VMEM((2, BANDS), f32),
            pltpu.VMEM((2, BANDS), f32),
            pltpu.VMEM((2, BANDS), f32),
            pltpu.SemaphoreType.DMA((GROUPS + 2,)),
            pltpu.SemaphoreType.DMA((9 * N_CHUNKS,)),
            pltpu.SemaphoreType.DMA((9 * N_CHUNKS,)),
            pltpu.SemaphoreType.DMA((6 * len(SETS),)),
            pltpu.SemaphoreType.DMA((6 * len(SETS),)),
            pltpu.SemaphoreType.DMA((RING - 1,)),
            pltpu.SemaphoreType.DMA((RING - 1,)),
            pltpu.SemaphoreType.DMA((1,)),
            pltpu.SemaphoreType.DMA((1,)),
            pltpu.SemaphoreType.REGULAR((2,)),
        ],
        compiler_params=pltpu.CompilerParams(
            collective_id=0, has_side_effects=True, vmem_limit_bytes=48 << 20
        ),
        name="momentum_step",
    )(gradients, momentum, basis)


def solution(mesh):
    return jax.shard_map(
        shards,
        mesh=mesh,
        in_specs=(P("rep", "fsdp", None, None), P("rep", "fsdp", None)),
        out_specs=(P("rep", "fsdp", None), P("fsdp", None)),
        check_vma=False,
    )
```

time: 58.5 us -> 46.5 us (0.79)
  Pallas kernels: 53.3 us -> 41.2 us
    pallas_call x1, Pallas kernels: 53.3 us -> 41.2 us  [shards(): pl.pallas_call(kernel, out_shape=(jax.ShapeDtypeStruct((1, 2, D), f32), j...]
where the time goes in v2:
time: 46.5 us; the launch traced here: 46.3 us
  Pallas kernels  41.2 us (89%)
  local copies, waits for them, and re-layouts  4.37 us (9%)
  between operations  0.65 us (1%)
    pallas_call x1, Pallas kernels, shards(): pl.pallas_call(kernel, out_shape=(jax.ShapeDtypeStruct((1, 2, D), f32), j...  41.2 us
    unnamed x8, local copies, waits for them, and re-layouts  4.37 us

profile of v2, /device:TPU:1, one launch (start us, length us, event | category | flops | bytes accessed | tf_op | source)
XLA Modules:
  0.0 46.3 jit_solution(14453424127129775208)
XLA Ops:
  0.6 0.0 copy-start
  0.6 1.3 %copy-done = bf16[1,1,128,5120]{3,2,1,0:T(8,128)(2,1)S(1)} copy-done((bf16[1,1,128,5120]{3,2,1,0:T(8,128)(2,1)S(1)}, bf16[1,1,128,5120]{3,2,1,0:T(8,128)(2,1)}, u32[]{:S(2)}) %copy-start) | copy-done | bytes 1310744
  1.9 0.0 copy-start.1
  1.9 1.0 %copy-done.1 = bf16[1024,256]{1,0:T(8,128)(2,1)S(1)} copy-done((bf16[1024,256]{1,0:T(8,128)(2,1)S(1)}, bf16[1024,256]{1,0:T(8,128)(2,1)}, u32[]{:S(2)}) %copy-start.1) | copy-done | bytes 524312
  3.0 0.0 copy-start.2
  3.0 0.8 %copy-done.2 = f32[1,2,5120]{2,1,0:T(2,128)S(1)} copy-done((f32[1,2,5120]{2,1,0:T(2,128)S(1)}, f32[1,2,5120]{2,1,0:T(2,128)}, u32[]{:S(2)}) %copy-start.2) | copy-done | bytes 40984
  3.8 41.2 %momentum_step.1 = (f32[1,2,5120]{2,1,0:T(2,128)S(1)}, f32[2,5120]{1,0:T(2,128)S(1)}) custom-call(bf16[1,1,128,5120]{3,2,1,0:T(8,128)(2,1)S(1)} %copy-done, f32[1,2,5120]{2,1,0:T(2,128)S(1)} %copy-done.2, bf16[1024,256]{1,0:T(8,128)(2,1)S(1)} %copy-done.1), custom_call_target="tpu_custom_call" | custom-call | tf_op jit(solution)/shard_map/momentum_step/pallas_call | solution.py:379
  45.0 0.6 %copy.7 = f32[1,2,5120]{2,1,0:T(2,128)} copy(f32[1,2,5120]{2,1,0:T(2,128)S(1)} %get-tuple-element.4) | data formatting | bytes 81920
  45.6 0.6 %copy.8 = f32[2,5120]{1,0:T(2,128)} copy(f32[2,5120]{1,0:T(2,128)S(1)} %get-tuple-element.5) | data formatting | bytes 81920
Async XLA Ops:
  0.6 1.3 %copy-start = (bf16[1,1,128,5120]{3,2,1,0:T(8,128)(2,1)S(1)}, bf16[1,1,128,5120]{3,2,1,0:T(8,128)(2,1)}, u32[]{:S(2)}) copy-start(bf16[1,1,128,5120]{3,2,1,0:T(8,128)(2,1)} %g_hbm.1) | copy-start | bytes 3932164
  1.9 1.0 %copy-start.1 = (bf16[1024,256]{1,0:T(8,128)(2,1)S(1)}, bf16[1024,256]{1,0:T(8,128)(2,1)}, u32[]{:S(2)}) copy-start(bf16[1024,256]{1,0:T(8,128)(2,1)} %constant.2.clone.b_hbm) | copy-start | bytes 1572868
  3.0 0.8 %copy-start.2 = (f32[1,2,5120]{2,1,0:T(2,128)S(1)}, f32[1,2,5120]{2,1,0:T(2,128)}, u32[]{:S(2)}) copy-start(f32[1,2,5120]{2,1,0:T(2,128)} %m_hbm.1) | copy-start | bytes 122884

commit v3 on v2

--- a/solution.py
+++ b/solution.py
@@ -20,11 +20,11 @@
 RING = 16
 
 CHUNKS = (
-    ("xyz", 0, 512),
-    ("yxz", 512, 512),
-    ("zxy", 1024, 512),
-    ("xyz", 1536, 896),
-    ("yxz", 2432, 896),
+    ("xyz", 0, 896),
+    ("yxz", 896, 896),
+    ("zxy", 1792, 512),
+    ("xyz", 2304, 512),
+    ("yxz", 2816, 512),
     ("xyz", 3328, 896),
     ("yxz", 4224, 896),
 )
@@ -46,17 +46,36 @@
     return np.concatenate([high, low], axis=1)
 
 
+def half(width):
+    return (width // 128 + 1) // 2 * 128
+
+
+def selector(source):
+    column = lax.broadcasted_iota(jnp.int32, (ROWS, ROWS), 1)
+    return jnp.where(source == column, 1.0, 0.0).astype(jnp.bfloat16)
+
+
+WEIGHT = {"y": 32, "z": 8, "x": 2}
+
+
 def permutation(order):
-    weight = {"y": 32, "z": 8, "x": 2}
     row = lax.broadcasted_iota(jnp.int32, (ROWS, ROWS), 0)
-    column = lax.broadcasted_iota(jnp.int32, (ROWS, ROWS), 1)
-    source = (
-        ((row >> 5) & 3) * weight[order[0]]
-        + ((row >> 3) & 3) * weight[order[1]]
-        + ((row >> 1) & 3) * weight[order[2]]
+    return selector(
+        ((row >> 5) & 3) * WEIGHT[order[0]]
+        + ((row >> 3) & 3) * WEIGHT[order[1]]
+        + ((row >> 1) & 3) * WEIGHT[order[2]]
         + (row & 1)
     )
-    return jnp.where(source == column, 1.0, 0.0).astype(jnp.bfloat16)
+
+
+def band_permutation(order):
+    row = lax.broadcasted_iota(jnp.int32, (ROWS, ROWS), 0)
+    return selector(
+        ((row >> 4) & 3) * WEIGHT[order[0]]
+        + ((row >> 2) & 3) * WEIGHT[order[1]]
+        + (row & 3) * WEIGHT[order[2]]
+        + (row >> 6)
+    )
 
 
 def split(value):
@@ -90,9 +109,9 @@
     scratch = list(scratch)
     take = lambda n: [scratch.pop(0) for _ in range(n)]
     g_ref, m_ref, b_ref, stack, band_stack = take(5)
-    per = take(6 * N_CHUNKS)
-    low_per = take(4 * len(SETS))
-    ring_out, ring_in, pair_out, pair_in, old_ref = take(5)
+    per = take(8 * N_CHUNKS)
+    low_per = take(6 * len(SETS))
+    ring_out, ring_in, pair_out, pair_in, old_ref, old_in = take(6)
     load_sems, send_sems, recv_sems, low_send, low_recv = take(5)
     ring_send, ring_recv, pair_send, pair_recv, relay = take(5)
 
@@ -148,35 +167,68 @@
             device_id_type=MESH,
         )
 
+    def rows(place, count):
+        return pl.ds(pl.multiple_of(place * count, count), count)
+
     def copies(c, phase):
-        order = CHUNKS[c][0]
-        t_ref, s_ref, u_ref, r1, r2, r3 = per[6 * c : 6 * c + 6]
+        order, first, width = CHUNKS[c]
+        t_ref, s_ref, u_ref, r1, r2, r3, ra, rb = per[8 * c : 8 * c + 8]
         result = []
         for k in (2, 1, 3):
             there, device = peer(order[phase], k)
             if phase == 0:
-                source, target = t_ref.at[pl.ds(pl.multiple_of(there * 32, 32), 32)], r1.at[k - 1]
+                source, target = t_ref.at[rows(there, 32)], r1.at[k - 1]
             elif phase == 1:
-                source, target = s_ref.at[pl.ds(pl.multiple_of(there * 8, 8), 8)], r2.at[k - 1]
+                source, target = s_ref.at[rows(there, 8)], r2.at[k - 1]
             else:
                 source, target = u_ref.at[there], r3.at[k - 1]
-            index = (c * 3 + phase) * 3 + k - 1
+            index = c * 12 + (phase * 3 + 3 if phase else 0) + k - 1
             result.append(remote(source, target, send_sems, recv_sems, index, device))
         return result
 
+    def hops(c, step, begin=0, end=4):
+        order, first, width = CHUNKS[c]
+        t_ref, s_ref, u_ref, r1, r2, r3, ra, rb = per[8 * c : 8 * c + 8]
+        cut = half(width)
+        one, two = pl.ds(0, cut), pl.ds(cut, width - cut)
+        far = peer(order[0], 2)[0]
+        after, up = peer(order[0], 1)
+        before, down = peer(order[0], 3)
+        if step == 0:
+            moves = [
+                (t_ref.at[rows(far, 32), one], ra, up),
+                (t_ref.at[rows(far, 32), two], rb, down),
+                (t_ref.at[rows(after, 32), two], r1.at[0, :, two], up),
+                (t_ref.at[rows(before, 32), one], r1.at[1, :, one], down),
+            ]
+        else:
+            moves = [
+                (t_ref.at[rows(after, 32), one], r1.at[0, :, one], up),
+                (t_ref.at[rows(before, 32), two], r1.at[1, :, two], down),
+            ]
+        return [
+            remote(source, target, send_sems, recv_sems, c * 12 + step * 4 + j, device)
+            for j, (source, target, device) in enumerate(moves)
+            if begin <= j < end
+        ]
+
     def low_copies(n, phase):
         order = SETS[n][0]
-        l_ref, s_ref, r1, r2 = low_per[4 * n : 4 * n + 4]
+        l_ref, k_ref, v_ref, s_ref, r1, r2 = low_per[6 * n : 6 * n + 6]
         result = []
         for k in (2, 1, 3):
             there, device = peer(order[phase], k)
             if phase == 0:
-                source, target = l_ref.at[pl.ds(pl.multiple_of(there * 32, 32), 32)], r1.at[k - 1]
+                source, target = v_ref.at[rows(there, 16)], r1.at[k - 1]
             else:
-                source, target = s_ref.at[pl.ds(pl.multiple_of(there * 8, 8), 8)], r2.at[k - 1]
+                source, target = s_ref.at[there], r2.at[k - 1]
             index = (n * 2 + phase) * 3 + k - 1
             result.append(remote(source, target, low_send, low_recv, index, device))
         return result
+
+    def swap_copy(n):
+        l_ref, k_ref = low_per[6 * n : 6 * n + 2]
+        return remote(l_ref.at[rows(1 - core, 64)], k_ref, pair_send, pair_recv, n + 1, other)
 
     def ring_copies():
         result = []
@@ -187,6 +239,9 @@
             )
         return result
 
+    def old_copy():
+        return remote(old_ref.at[1 - core], old_in, pair_send, pair_recv, len(SETS) + 1, other)
+
     def pair_copy():
         return remote(pair_out, pair_in, pair_send, pair_recv, 0, other)
 
@@ -200,50 +255,71 @@
 
     def turn(c):
         order, first, width = CHUNKS[c]
-        per[6 * c][...] = jnp.dot(
+        per[8 * c][...] = jnp.dot(
             turned[order], g_ref[:, first : first + width], preferred_element_type=jnp.float32
         )
 
     def low_first(n):
         order, first, count = SETS[n]
+        place = band_permutation(order)
         for j in range(count):
             begin = (first + j) * GROUP
-            loads[first + j].wait()
             both = jnp.dot(
                 g_ref[:, begin : begin + GROUP], b_ref[...], preferred_element_type=jnp.float32
             )
             high, low = split(both[:, :128] + both[:, 128:])
-            low_per[4 * n][:, j * 128 : (j + 1) * 128] = jnp.dot(
-                turned[order], high, preferred_element_type=jnp.float32
-            ) + jnp.dot(turned[order], low, preferred_element_type=jnp.float32)
+            low_per[6 * n][:, j * 128 : (j + 1) * 128] = jnp.dot(
+                place, high, preferred_element_type=jnp.float32
+            ) + jnp.dot(place, low, preferred_element_type=jnp.float32)
+        swap_copy(n).start()
+
+    def low_swapped(n):
+        l_ref, k_ref, v_ref, s_ref, r1, r2 = low_per[6 * n : 6 * n + 6]
+        arrive([swap_copy(n)])
+        v_ref[...] = l_ref[rows(core, 64), :] + k_ref[...]
+        start(low_copies(n, 0))
 
     def low_second(n):
-        l_ref, s_ref, r1, r2 = low_per[4 * n : 4 * n + 4]
+        l_ref, k_ref, v_ref, s_ref, r1, r2 = low_per[6 * n : 6 * n + 6]
         arrive(low_copies(n, 0))
-        own = pl.ds(pl.multiple_of(at[SETS[n][0][0]] * 32, 32), 32)
-        s_ref[...] = (l_ref[own, :] + r1[0]) + (r1[1] + r1[2])
+        total = (v_ref[rows(at[SETS[n][0][0]], 16), :] + r1[0]) + (r1[1] + r1[2])
+        for q in range(4):
+            s_ref[q] = total[4 * q : 4 * q + 4]
         start(low_copies(n, 1))
 
     def low_third(n):
-        l_ref, s_ref, r1, r2 = low_per[4 * n : 4 * n + 4]
+        l_ref, k_ref, v_ref, s_ref, r1, r2 = low_per[6 * n : 6 * n + 6]
         order, first, count = SETS[n]
         arrive(low_copies(n, 1))
-        own = pl.ds(pl.multiple_of(at[order[1]] * 8, 8), 8)
-        total = (s_ref[own, :] + r2[0]) + (r2[1] + r2[2])
+        total = (s_ref[at[order[1]]] + r2[0]) + (r2[1] + r2[2])
         for q in range(4):
-            ring_out[q, :, first * 128 : (first + count) * 128] = total[2 * q : 2 * q + 2]
+            ring_out[q, :, first * 128 : (first + count) * 128] = total[q : q + 1]
+
+    def relayed(c):
+        order, first, width = CHUNKS[c]
+        t_ref, s_ref, u_ref, r1, r2, r3, ra, rb = per[8 * c : 8 * c + 8]
+        cut = half(width)
+        arrive(hops(c, 0, 0, 2))
+        after, before = rows(peer(order[0], 1)[0], 32), rows(peer(order[0], 3)[0], 32)
+        t_ref[after, :cut] = t_ref[after, :cut] + ra[...]
+        t_ref[before, cut:] = t_ref[before, cut:] + rb[...]
+        start(hops(c, 1))
 
     def second(c):
         order, first, width = CHUNKS[c]
-        t_ref, s_ref, u_ref, r1, r2, r3 = per[6 * c : 6 * c + 6]
-        arrive(copies(c, 0))
-        own = pl.ds(pl.multiple_of(at[order[0]] * 32, 32), 32)
-        s_ref[...] = (t_ref[own, :] + r1[0]) + (r1[1] + r1[2])
+        t_ref, s_ref, u_ref, r1, r2, r3, ra, rb = per[8 * c : 8 * c + 8]
+        own = rows(at[order[0]], 32)
+        if order[0] == "z":
+            arrive(copies(c, 0))
+            s_ref[...] = (t_ref[own, :] + r1[0]) + (r1[1] + r1[2])
+        else:
+            arrive(hops(c, 0, 2) + hops(c, 1))
+            s_ref[...] = t_ref[own, :] + (r1[0] + r1[1])
         start(copies(c, 1))
 
     def third(c):
         order, first, width = CHUNKS[c]
-        t_ref, s_ref, u_ref, r1, r2, r3 = per[6 * c : 6 * c + 6]
+        t_ref, s_ref, u_ref, r1, r2, r3, ra, rb = per[8 * c : 8 * c + 8]
         arrive(copies(c, 1))
         own = pl.ds(pl.multiple_of(at[order[1]] * 8, 8), 8)
         total = (s_ref[own, :] + r2[0]) + (r2[1] + r2[2])
@@ -253,7 +329,7 @@
 
     def last(c):
         order, first, width = CHUNKS[c]
-        t_ref, s_ref, u_ref, r1, r2, r3 = per[6 * c : 6 * c + 6]
+        t_ref, s_ref, u_ref, r1, r2, r3, ra, rb = per[8 * c : 8 * c + 8]
         arrive(copies(c, 2))
         total = (u_ref[at[order[2]]] + r3[0]) + (r3[1] + r3[2])
         blended = DECAY * m_ref[:, first : first + width] + total
@@ -280,17 +356,26 @@
                 relay.at[j], inc=1, device_id=ring_peer(k)[1], device_id_type=MESH
             )
 
-    b_load.wait()
-    for n in range(len(SETS)):
-        low_first(n)
-    for c in range(3):
-        turn(c)
+    loads[0].wait()
+    turn(0)
     pl.semaphore_wait(barrier, len(greeted))
     relay_signal(0)
-    for n in range(len(SETS)):
-        start(low_copies(n, 0))
-    for c in range(3):
-        start(copies(c, 0))
+    start(hops(0, 0))
+    loads[1].wait()
+    turn(1)
+    start(hops(1, 0))
+    loads[2].wait()
+    turn(2)
+    start(copies(2, 0))
+    b_load.wait()
+    low_first(0)
+    loads[3].wait()
+    loads[4].wait()
+    low_first(1)
+    low_swapped(0)
+    low_swapped(1)
+    for c in range(3, N_CHUNKS):
+        turn(c)
     m_load.wait()
     high, low = b_ref[:, :128], b_ref[:, 128:]
     old = DECAY * m_ref[...]
@@ -298,46 +383,55 @@
         stack[2 * g : 2 * g + 2, :] = old[:, g * GROUP : (g + 1) * GROUP]
     old_band = analyse(stack[...], high, low)
     for g in range(GROUPS):
-        old_ref[:, g * 128 : (g + 1) * 128] = old_band[2 * g : 2 * g + 2]
-    for c in range(3, N_CHUNKS):
-        turn(c)
+        for i in range(2):
+            old_ref[i, :, g * 128 : (g + 1) * 128] = old_band[2 * g + i : 2 * g + i + 1]
+    start([old_copy()])
+    pl.semaphore_wait(relay.at[0], 2)
+    relay_signal(1)
+    relayed(0)
+    relayed(1)
+    start(hops(3, 0))
+    start(hops(4, 0))
     for n in range(len(SETS)):
         low_second(n)
-    for c in (3, 4):
-        start(copies(c, 0))
-    pl.semaphore_wait(relay.at[0], 2)
-    relay_signal(1)
+    start(hops(5, 0))
+    start(hops(6, 0))
+    relayed(3)
+    relayed(4)
+    for n in range(len(SETS)):
+        low_third(n)
+    arrive([old_copy()])
+    ring_out[at["z"]] = ring_out[at["z"]] + (old_ref[core] + old_in[...])
+    pl.semaphore_wait(relay.at[1], 2)
+    start(ring_copies())
     second(0)
     second(1)
-    for c in (5, 6):
-        start(copies(c, 0))
-    for n in range(len(SETS)):
-        low_third(n)
-    ring_out[at["z"]] = ring_out[at["z"]] + old_ref[...]
-    pl.semaphore_wait(relay.at[1], 2)
-    start(ring_copies())
     second(2)
+    relayed(5)
+    relayed(6)
+    third(0)
+    third(1)
     second(3)
     second(4)
-    third(0)
-    third(1)
     third(2)
     second(5)
     second(6)
+    last(0)
+    last(1)
     third(3)
     third(4)
-    last(0)
-    last(1)
     last(2)
+    low_fourth()
     third(5)
     third(6)
-    low_fourth()
     last(3)
     last(4)
     arrive([pair_copy()])
     for g in range(GROUPS):
         lanes = slice(g * 128, (g + 1) * 128)
-        band_stack[2 * g : 2 * g + 2, :] = pair_out[:, lanes] + pair_in[:, lanes]
+        mine, theirs = pair_out[:, lanes], pair_in[:, lanes]
+        band_stack[2 * g : 2 * g + 1, :] = jnp.where(core == 0, mine, theirs)
+        band_stack[2 * g + 1 : 2 * g + 2, :] = jnp.where(core == 0, theirs, mine)
     update = expand(band_stack[...] * (1.0 / REPS), high, low)
     for g in range(GROUPS):
         update_ref[:, g * GROUP : (g + 1) * GROUP] = update[2 * g : 2 * g + 2]
@@ -347,9 +441,12 @@
     fresh = blended - expand(analyse(blended, high, low), high, low)
     for g in range(GROUPS):
         fresh_ref[0, :, g * GROUP : (g + 1) * GROUP] = fresh[2 * g : 2 * g + 2]
-    sent = [copy for c in range(N_CHUNKS) for phase in range(3) for copy in copies(c, phase)]
+    sent = []
+    for c in range(N_CHUNKS):
+        sent += copies(c, 0) if CHUNKS[c][0][0] == "z" else hops(c, 0) + hops(c, 1)
+        sent += copies(c, 1) + copies(c, 2)
     sent += [copy for n in range(len(SETS)) for phase in range(2) for copy in low_copies(n, phase)]
-    sent += ring_copies() + [pair_copy()]
+    sent += ring_copies() + [pair_copy(), old_copy()] + [swap_copy(n) for n in range(len(SETS))]
     for copy in sent:
         copy.wait_send()
 
@@ -363,18 +460,22 @@
             pltpu.VMEM((ROWS, width), f32),
             pltpu.VMEM((32, width), f32),
             pltpu.VMEM((4, 2, width), f32),
-            pltpu.VMEM((3, 32, width), f32),
+            pltpu.VMEM((3 if order[0] == "z" else 2, 32, width), f32),
             pltpu.VMEM((3, 8, width), f32),
             pltpu.VMEM((3, 2, width), f32),
+            pltpu.VMEM((32, half(width)), f32),
+            pltpu.VMEM((32, width - half(width)), f32),
         ]
     low_per = []
     for order, first, count in SETS:
         width = count * 128
         low_per += [
             pltpu.VMEM((ROWS, width), f32),
-            pltpu.VMEM((32, width), f32),
-            pltpu.VMEM((3, 32, width), f32),
-            pltpu.VMEM((3, 8, width), f32),
+            pltpu.VMEM((64, width), f32),
+            pltpu.VMEM((64, width), f32),
+            pltpu.VMEM((4, 4, width), f32),
+            pltpu.VMEM((3, 16, width), f32),
+            pltpu.VMEM((3, 4, width), f32),
         ]
     return pl.pallas_call(
         kernel,
@@ -392,24 +493,25 @@
             pltpu.VMEM((16, 128), f32),
             *per,
             *low_per,
-            pltpu.VMEM((4, 2, BANDS), f32),
-            pltpu.VMEM((RING - 1, 2, BANDS), f32),
-            pltpu.VMEM((2, BANDS), f32),
-            pltpu.VMEM((2, BANDS), f32),
-            pltpu.VMEM((2, BANDS), f32),
+            pltpu.VMEM((4, 1, BANDS), f32),
+            pltpu.VMEM((RING - 1, 1, BANDS), f32),
+            pltpu.VMEM((1, BANDS), f32),
+            pltpu.VMEM((1, BANDS), f32),
+            pltpu.VMEM((2, 1, BANDS), f32),
+            pltpu.VMEM((1, BANDS), f32),
             pltpu.SemaphoreType.DMA((GROUPS + 2,)),
-            pltpu.SemaphoreType.DMA((9 * N_CHUNKS,)),
-            pltpu.SemaphoreType.DMA((9 * N_CHUNKS,)),
+            pltpu.SemaphoreType.DMA((12 * N_CHUNKS,)),
+            pltpu.SemaphoreType.DMA((12 * N_CHUNKS,)),
             pltpu.SemaphoreType.DMA((6 * len(SETS),)),
             pltpu.SemaphoreType.DMA((6 * len(SETS),)),
             pltpu.SemaphoreType.DMA((RING - 1,)),
             pltpu.SemaphoreType.DMA((RING - 1,)),
-            pltpu.SemaphoreType.DMA((1,)),
-            pltpu.SemaphoreType.DMA((1,)),
+            pltpu.SemaphoreType.DMA((len(SETS) + 2,)),
+            pltpu.SemaphoreType.DMA((len(SETS) + 2,)),
             pltpu.SemaphoreType.REGULAR((2,)),
         ],
         compiler_params=pltpu.CompilerParams(
-            collective_id=0, has_side_effects=True, vmem_limit_bytes=48 << 20
+            collective_id=0, has_side_effects=True, vmem_limit_bytes=107 << 19
         ),
         name="momentum_step",
     )(gradients, momentum, basis)

time: 46.5 us -> 42.3 us (0.910)
  local copies, waits for them, and re-layouts: 4.37 us -> 2.01 us
  Pallas kernels: 41.2 us -> 39.4 us
    unnamed x8 -> x4, local copies, waits for them, and re-layouts: 4.37 us -> 2.01 us
    pallas_call x1, Pallas kernels: 41.2 us -> 39.4 us  [shards(): pl.pallas_call(kernel, out_shape=(jax.ShapeDtypeStruct((1, 2, D), f32), j...]
where the time goes in v3:
time: 42.3 us; the launch traced here: 42.1 us
  Pallas kernels  39.4 us (93%)
  local copies, waits for them, and re-layouts  2.01 us (5%)
  between operations  0.65 us (2%)
    pallas_call x1, Pallas kernels, shards(): pl.pallas_call(kernel, out_shape=(jax.ShapeDtypeStruct((1, 2, D), f32), j...  39.4 us
    unnamed x4, local copies, waits for them, and re-layouts  2.01 us

profile of v3, /device:TPU:1, one launch (start us, length us, event | category | flops | bytes accessed | tf_op | source)
XLA Modules:
  0.0 42.1 jit_solution(7250348045042104626)
XLA Ops:
  0.6 0.0 copy-start
  0.6 0.8 %copy-done = f32[1,2,5120]{2,1,0:T(2,128)S(1)} copy-done((f32[1,2,5120]{2,1,0:T(2,128)S(1)}, f32[1,2,5120]{2,1,0:T(2,128)}, u32[]{:S(2)}) %copy-start) | copy-done | bytes 40984
  1.4 39.4 %momentum_step.1 = (f32[1,2,5120]{2,1,0:T(2,128)S(1)}, f32[2,5120]{1,0:T(2,128)S(1)}) custom-call(bf16[1,1,128,5120]{3,2,1,0:T(8,128)(2,1)} %g_hbm.1, f32[1,2,5120]{2,1,0:T(2,128)S(1)} %copy-done, bf16[1024,256]{1,0:T(8,128)(2,1)} %constant.2.clone.b_hbm), custom_call_target="tpu_custom_call" | custom-call | tf_op jit(solution)/shard_map/momentum_step/pallas_call | solution.py:480
  40.9 0.6 %copy.7 = f32[1,2,5120]{2,1,0:T(2,128)} copy(f32[1,2,5120]{2,1,0:T(2,128)S(1)} %get-tuple-element.4) | data formatting | bytes 81920
  41.5 0.6 %copy.8 = f32[2,5120]{1,0:T(2,128)} copy(f32[2,5120]{1,0:T(2,128)S(1)} %get-tuple-element.5) | data formatting | bytes 81920
Async XLA Ops:
  0.6 0.8 %copy-start = (f32[1,2,5120]{2,1,0:T(2,128)S(1)}, f32[1,2,5120]{2,1,0:T(2,128)}, u32[]{:S(2)}) copy-start(f32[1,2,5120]{2,1,0:T(2,128)} %m_hbm.1) | copy-start | bytes 122884

commit v4 on v3

--- a/solution.py
+++ b/solution.py
@@ -23,10 +23,10 @@
     ("xyz", 0, 896),
     ("yxz", 896, 896),
     ("zxy", 1792, 512),
-    ("xyz", 2304, 512),
-    ("yxz", 2816, 512),
-    ("xyz", 3328, 896),
-    ("yxz", 4224, 896),
+    ("xyz", 2304, 896),
+    ("yxz", 3200, 896),
+    ("xyz", 4096, 512),
+    ("yxz", 4608, 512),
 )
 N_CHUNKS = len(CHUNKS)
 SETS = (("xyz", 0, 2), ("yxz", 2, 3))
@@ -133,12 +133,27 @@
 
     other = {"rep": rep + 1 - 2 * core, "fsdp": fsdp}
 
+    cube, level = rep // 2, at["z"]
+    waits_down, waits_up = cube >= 1, cube == 3
+    crossing = [(k, level + k > 3, waits_up, cube < 3) for k in (1, 2, 3)]
+    crossing += [(-k, level < k, waits_down, cube == 0) for k in (1, 2, 3)]
+
+    def across(k):
+        return ring_peer((k + RING) % RING)[1]
+
     barrier = pltpu.get_barrier_semaphore()
-    greeted = [ring_peer(k)[1] for k in (3, 13, 2, 14, 1, 15)]
-    greeted += [peer(axis, k)[1] for k in (2, 1, 3) for axis in "xy"]
-    greeted.append(other)
-    for device in greeted:
-        pl.semaphore_signal(barrier, inc=1, device_id=device, device_id_type=MESH)
+    for k, crosses, mine, theirs in crossing:
+
+        @pl.when(jnp.logical_and(crosses, theirs))
+        def _():
+            pl.semaphore_signal(barrier, inc=1, device_id=across(k), device_id_type=MESH)
+
+    for k in (2, 1, 3):
+        for axis in "zxy":
+            pl.semaphore_signal(barrier, inc=1, device_id=peer(axis, k)[1], device_id_type=MESH)
+    pl.semaphore_signal(barrier, inc=1, device_id=other, device_id_type=MESH)
+    entry = 10 + jnp.where(waits_down, 3 - level, 0) + jnp.where(waits_up, level, 0)
+    greetings = jnp.where(waits_down, 0, 3 - level) + jnp.where(waits_up, 0, level)
 
     loads = []
     for g in range(GROUPS):
@@ -262,15 +277,17 @@
     def low_first(n):
         order, first, count = SETS[n]
         place = band_permutation(order)
+        parts = []
         for j in range(count):
             begin = (first + j) * GROUP
             both = jnp.dot(
                 g_ref[:, begin : begin + GROUP], b_ref[...], preferred_element_type=jnp.float32
             )
-            high, low = split(both[:, :128] + both[:, 128:])
-            low_per[6 * n][:, j * 128 : (j + 1) * 128] = jnp.dot(
-                place, high, preferred_element_type=jnp.float32
-            ) + jnp.dot(place, low, preferred_element_type=jnp.float32)
+            parts.append(both[:, :128] + both[:, 128:])
+        high, low = split(jnp.concatenate(parts, axis=1))
+        low_per[6 * n][...] = jnp.dot(place, high, preferred_element_type=jnp.float32) + jnp.dot(
+            place, low, preferred_element_type=jnp.float32
+        )
         swap_copy(n).start()
 
     def low_swapped(n):
@@ -356,10 +373,34 @@
                 relay.at[j], inc=1, device_id=ring_peer(k)[1], device_id_type=MESH
             )
 
+    def greet():
+        for k, crosses, mine, theirs in crossing:
+
+            @pl.when(jnp.logical_and(crosses, mine))
+            def _():
+                pl.semaphore_signal(relay.at[2], inc=1, device_id=across(k), device_id_type=MESH)
+
+    def stage(number, when):
+        @pl.when(when)
+        def _():
+            if number == 0:
+                @pl.when(greetings > 0)
+                def _():
+                    pl.semaphore_wait(relay.at[2], greetings)
+
+                relay_signal(0)
+            elif number == 1:
+                pl.semaphore_wait(relay.at[0], 2)
+                relay_signal(1)
+            else:
+                pl.semaphore_wait(relay.at[1], 2)
+                start(ring_copies())
+
+    early, late = cube > 0, cube == 0
     loads[0].wait()
     turn(0)
-    pl.semaphore_wait(barrier, len(greeted))
-    relay_signal(0)
+    pl.semaphore_wait(barrier, entry)
+    greet()
     start(hops(0, 0))
     loads[1].wait()
     turn(1)
@@ -374,6 +415,7 @@
     low_first(1)
     low_swapped(0)
     low_swapped(1)
+    stage(0, early)
     for c in range(3, N_CHUNKS):
         turn(c)
     m_load.wait()
@@ -386,33 +428,34 @@
         for i in range(2):
             old_ref[i, :, g * 128 : (g + 1) * 128] = old_band[2 * g + i : 2 * g + i + 1]
     start([old_copy()])
-    pl.semaphore_wait(relay.at[0], 2)
-    relay_signal(1)
     relayed(0)
     relayed(1)
     start(hops(3, 0))
     start(hops(4, 0))
     for n in range(len(SETS)):
         low_second(n)
+    stage(1, early)
     start(hops(5, 0))
     start(hops(6, 0))
     relayed(3)
     relayed(4)
+    stage(0, late)
     for n in range(len(SETS)):
         low_third(n)
     arrive([old_copy()])
     ring_out[at["z"]] = ring_out[at["z"]] + (old_ref[core] + old_in[...])
-    pl.semaphore_wait(relay.at[1], 2)
-    start(ring_copies())
     second(0)
     second(1)
+    stage(2, early)
     second(2)
+    stage(1, late)
     relayed(5)
     relayed(6)
     third(0)
     third(1)
     second(3)
     second(4)
+    stage(2, late)
     third(2)
     second(5)
     second(6)
@@ -421,11 +464,17 @@
     third(3)
     third(4)
     last(2)
-    low_fourth()
     third(5)
     third(6)
     last(3)
     last(4)
+    low_fourth()
+    last(5)
+    last(6)
+    blended = stack[...]
+    fresh = blended - expand(analyse(blended, high, low), high, low)
+    for g in range(GROUPS):
+        fresh_ref[0, :, g * GROUP : (g + 1) * GROUP] = fresh[2 * g : 2 * g + 2]
     arrive([pair_copy()])
     for g in range(GROUPS):
         lanes = slice(g * 128, (g + 1) * 128)
@@ -435,12 +484,6 @@
     update = expand(band_stack[...] * (1.0 / REPS), high, low)
     for g in range(GROUPS):
         update_ref[:, g * GROUP : (g + 1) * GROUP] = update[2 * g : 2 * g + 2]
-    last(5)
-    last(6)
-    blended = stack[...]
-    fresh = blended - expand(analyse(blended, high, low), high, low)
-    for g in range(GROUPS):
-        fresh_ref[0, :, g * GROUP : (g + 1) * GROUP] = fresh[2 * g : 2 * g + 2]
     sent = []
     for c in range(N_CHUNKS):
         sent += copies(c, 0) if CHUNKS[c][0][0] == "z" else hops(c, 0) + hops(c, 1)
@@ -508,10 +551,10 @@
             pltpu.SemaphoreType.DMA((RING - 1,)),
             pltpu.SemaphoreType.DMA((len(SETS) + 2,)),
             pltpu.SemaphoreType.DMA((len(SETS) + 2,)),
-            pltpu.SemaphoreType.REGULAR((2,)),
+            pltpu.SemaphoreType.REGULAR((3,)),
         ],
         compiler_params=pltpu.CompilerParams(
-            collective_id=0, has_side_effects=True, vmem_limit_bytes=107 << 19
+            collective_id=0, has_side_effects=True, vmem_limit_bytes=55136 << 10
         ),
         name="momentum_step",
     )(gradients, momentum, basis)

time: 42.3 us -> 38.6 us (0.913)
  Pallas kernels: 39.4 us -> 36.6 us
  local copies, waits for them, and re-layouts: 2.01 us -> 1.24 us
    pallas_call x1, Pallas kernels: 39.4 us -> 36.6 us  [shards(): pl.pallas_call(kernel, out_shape=(jax.ShapeDtypeStruct((1, 2, D), f32), j...]
    unnamed x4 -> x2, local copies, waits for them, and re-layouts: 2.01 us -> 1.24 us
where the time goes in v4:
time: 38.6 us; the launch traced here: 38.5 us
  Pallas kernels  36.6 us (95%)
  local copies, waits for them, and re-layouts  1.24 us (3%)
  between operations  0.64 us (2%)
    pallas_call x1, Pallas kernels, shards(): pl.pallas_call(kernel, out_shape=(jax.ShapeDtypeStruct((1, 2, D), f32), j...  36.6 us
    unnamed x2, local copies, waits for them, and re-layouts  1.24 us

profile of v4, /device:TPU:1, one launch (start us, length us, event | category | flops | bytes accessed | tf_op | source)
XLA Modules:
  0.0 38.5 jit_solution(42749991194327285)
XLA Ops:
  0.6 36.6 %momentum_step.1 = (f32[1,2,5120]{2,1,0:T(2,128)S(1)}, f32[2,5120]{1,0:T(2,128)S(1)}) custom-call(bf16[1,1,128,5120]{3,2,1,0:T(8,128)(2,1)} %g_hbm.1, f32[1,2,5120]{2,1,0:T(2,128)} %m_hbm.1, bf16[1024,256]{1,0:T(8,128)(2,1)} %constant.2.clone.b_hbm), custom_call_target="tpu_custom_call" | custom-call | tf_op jit(solution)/shard_map/momentum_step/pallas_call | solution.py:523
  37.3 0.6 %copy.7 = f32[1,2,5120]{2,1,0:T(2,128)} copy(f32[1,2,5120]{2,1,0:T(2,128)S(1)} %get-tuple-element.4) | data formatting | bytes 81920
  37.9 0.6 %copy.8 = f32[2,5120]{1,0:T(2,128)} copy(f32[2,5120]{1,0:T(2,128)S(1)} %get-tuple-element.5) | data formatting | bytes 81920

commit v5 on v4

--- a/solution.py
+++ b/solution.py
@@ -22,9 +22,9 @@
 CHUNKS = (
     ("xyz", 0, 896),
     ("yxz", 896, 896),
-    ("zxy", 1792, 512),
-    ("xyz", 2304, 896),
-    ("yxz", 3200, 896),
+    ("zxy", 1792, 768),
+    ("xyz", 2560, 768),
+    ("yxz", 3328, 768),
     ("xyz", 4096, 512),
     ("yxz", 4608, 512),
 )
@@ -444,9 +444,9 @@
         low_third(n)
     arrive([old_copy()])
     ring_out[at["z"]] = ring_out[at["z"]] + (old_ref[core] + old_in[...])
+    stage(2, early)
     second(0)
     second(1)
-    stage(2, early)
     second(2)
     stage(1, late)
     relayed(5)
@@ -466,9 +466,9 @@
     last(2)
     third(5)
     third(6)
+    low_fourth()
     last(3)
     last(4)
-    low_fourth()
     last(5)
     last(6)
     blended = stack[...]

time: 38.6 us -> 38.3 us (level)
  no operation moved by 1% of the time
where the time goes in v5:
time: 38.3 us; the launch traced here: 38.1 us
  Pallas kernels  36.3 us (95%)
  local copies, waits for them, and re-layouts  1.24 us (3%)
  between operations  0.64 us (2%)
    pallas_call x1, Pallas kernels, shards(): pl.pallas_call(kernel, out_shape=(jax.ShapeDtypeStruct((1, 2, D), f32), j...  36.3 us
    unnamed x2, local copies, waits for them, and re-layouts  1.24 us

profile of v5, /device:TPU:1, one launch (start us, length us, event | category | flops | bytes accessed | tf_op | source)
XLA Modules:
  0.0 38.1 jit_solution(16859551101914587105)
XLA Ops:
  0.6 36.3 %momentum_step.1 = (f32[1,2,5120]{2,1,0:T(2,128)S(1)}, f32[2,5120]{1,0:T(2,128)S(1)}) custom-call(bf16[1,1,128,5120]{3,2,1,0:T(8,128)(2,1)} %g_hbm.1, f32[1,2,5120]{2,1,0:T(2,128)} %m_hbm.1, bf16[1024,256]{1,0:T(8,128)(2,1)} %constant.2.clone.b_hbm), custom_call_target="tpu_custom_call" | custom-call | tf_op jit(solution)/shard_map/momentum_step/pallas_call | solution.py:523
  36.9 0.6 %copy.7 = f32[1,2,5120]{2,1,0:T(2,128)} copy(f32[1,2,5120]{2,1,0:T(2,128)S(1)} %get-tuple-element.4) | data formatting | bytes 81920
  37.5 0.6 %copy.8 = f32[2,5120]{1,0:T(2,128)} copy(f32[2,5120]{1,0:T(2,128)S(1)} %get-tuple-element.5) | data formatting | bytes 81920

commit v6 on v5

--- a/solution.py
+++ b/solution.py
@@ -23,10 +23,10 @@
     ("xyz", 0, 896),
     ("yxz", 896, 896),
     ("zxy", 1792, 768),
-    ("xyz", 2560, 768),
-    ("yxz", 3328, 768),
-    ("xyz", 4096, 512),
-    ("yxz", 4608, 512),
+    ("xyz", 2560, 896),
+    ("yxz", 3456, 896),
+    ("xyz", 4352, 384),
+    ("yxz", 4736, 384),
 )
 N_CHUNKS = len(CHUNKS)
 SETS = (("xyz", 0, 2), ("yxz", 2, 3))

time: 38.3 us -> 38.7 us (1.010)
  Pallas kernels: 36.3 us -> 36.7 us
    pallas_call x1, Pallas kernels: 36.3 us -> 36.7 us  [shards(): pl.pallas_call(kernel, out_shape=(jax.ShapeDtypeStruct((1, 2, D), f32), j...]
where the time goes in v6:
time: 38.7 us; the launch traced here: 38.5 us
  Pallas kernels  36.7 us (95%)
  local copies, waits for them, and re-layouts  1.24 us (3%)
  between operations  0.64 us (2%)
    pallas_call x1, Pallas kernels, shards(): pl.pallas_call(kernel, out_shape=(jax.ShapeDtypeStruct((1, 2, D), f32), j...  36.7 us
    unnamed x2, local copies, waits for them, and re-layouts  1.24 us

profile of v6, /device:TPU:1, one launch (start us, length us, event | category | flops | bytes accessed | tf_op | source)
XLA Modules:
  0.0 38.5 jit_solution(18177081281543731977)
XLA Ops:
  0.6 36.7 %momentum_step.1 = (f32[1,2,5120]{2,1,0:T(2,128)S(1)}, f32[2,5120]{1,0:T(2,128)S(1)}) custom-call(bf16[1,1,128,5120]{3,2,1,0:T(8,128)(2,1)} %g_hbm.1, f32[1,2,5120]{2,1,0:T(2,128)} %m_hbm.1, bf16[1024,256]{1,0:T(8,128)(2,1)} %constant.2.clone.b_hbm), custom_call_target="tpu_custom_call" | custom-call | tf_op jit(solution)/shard_map/momentum_step/pallas_call | solution.py:523
  37.3 0.6 %copy.7 = f32[1,2,5120]{2,1,0:T(2,128)} copy(f32[1,2,5120]{2,1,0:T(2,128)S(1)} %get-tuple-element.4) | data formatting | bytes 81920
  37.9 0.6 %copy.8 = f32[2,5120]{1,0:T(2,128)} copy(f32[2,5120]{1,0:T(2,128)S(1)} %get-tuple-element.5) | data formatting | bytes 81920

commit v7 on v5

--- a/solution.py
+++ b/solution.py
@@ -22,9 +22,9 @@
 CHUNKS = (
     ("xyz", 0, 896),
     ("yxz", 896, 896),
-    ("zxy", 1792, 768),
-    ("xyz", 2560, 768),
-    ("yxz", 3328, 768),
+    ("zxy", 1792, 1024),
+    ("xyz", 2816, 640),
+    ("yxz", 3456, 640),
     ("xyz", 4096, 512),
     ("yxz", 4608, 512),
 )

time: 38.3 us -> 38 us (level)
  no operation moved by 1% of the time
where the time goes in v7:
time: 38 us; the launch traced here: 37.9 us
  Pallas kernels  36 us (95%)
  local copies, waits for them, and re-layouts  1.24 us (3%)
  between operations  0.64 us (2%)
    pallas_call x1, Pallas kernels, shards(): pl.pallas_call(kernel, out_shape=(jax.ShapeDtypeStruct((1, 2, D), f32), j...  36 us
    unnamed x2, local copies, waits for them, and re-layouts  1.24 us

profile of v7, /device:TPU:1, one launch (start us, length us, event | category | flops | bytes accessed | tf_op | source)
XLA Modules:
  0.0 37.9 jit_solution(7654962001094431378)
XLA Ops:
  0.6 36.0 %momentum_step.1 = (f32[1,2,5120]{2,1,0:T(2,128)S(1)}, f32[2,5120]{1,0:T(2,128)S(1)}) custom-call(bf16[1,1,128,5120]{3,2,1,0:T(8,128)(2,1)} %g_hbm.1, f32[1,2,5120]{2,1,0:T(2,128)} %m_hbm.1, bf16[1024,256]{1,0:T(8,128)(2,1)} %constant.2.clone.b_hbm), custom_call_target="tpu_custom_call" | custom-call | tf_op jit(solution)/shard_map/momentum_step/pallas_call | solution.py:523
  36.6 0.6 %copy.7 = f32[1,2,5120]{2,1,0:T(2,128)} copy(f32[1,2,5120]{2,1,0:T(2,128)S(1)} %get-tuple-element.4) | data formatting | bytes 81920
  37.3 0.6 %copy.8 = f32[2,5120]{1,0:T(2,128)} copy(f32[2,5120]{1,0:T(2,128)S(1)} %get-tuple-element.5) | data formatting | bytes 81920

commit v8 on v7

--- a/solution.py
+++ b/solution.py
@@ -22,9 +22,9 @@
 CHUNKS = (
     ("xyz", 0, 896),
     ("yxz", 896, 896),
-    ("zxy", 1792, 1024),
-    ("xyz", 2816, 640),
-    ("yxz", 3456, 640),
+    ("zxy", 1792, 1280),
+    ("xyz", 3072, 512),
+    ("yxz", 3584, 512),
     ("xyz", 4096, 512),
     ("yxz", 4608, 512),
 )

time: 38 us -> 41 us (1.079)
  Pallas kernels: 36 us -> 39 us
    pallas_call x1, Pallas kernels: 36 us -> 39 us  [shards(): pl.pallas_call(kernel, out_shape=(jax.ShapeDtypeStruct((1, 2, D), f32), j...]
where the time goes in v8:
time: 41 us; the launch traced here: 40.9 us
  Pallas kernels  39 us (95%)
  local copies, waits for them, and re-layouts  1.24 us (3%)
  between operations  0.64 us (2%)
    pallas_call x1, Pallas kernels, shards(): pl.pallas_call(kernel, out_shape=(jax.ShapeDtypeStruct((1, 2, D), f32), j...  39 us
    unnamed x2, local copies, waits for them, and re-layouts  1.24 us

profile of v8, /device:TPU:1, one launch (start us, length us, event | category | flops | bytes accessed | tf_op | source)
XLA Modules:
  0.0 40.9 jit_solution(15456043180860952108)
XLA Ops:
  0.6 39.0 %momentum_step.1 = (f32[1,2,5120]{2,1,0:T(2,128)S(1)}, f32[2,5120]{1,0:T(2,128)S(1)}) custom-call(bf16[1,1,128,5120]{3,2,1,0:T(8,128)(2,1)} %g_hbm.1, f32[1,2,5120]{2,1,0:T(2,128)} %m_hbm.1, bf16[1024,256]{1,0:T(8,128)(2,1)} %constant.2.clone.b_hbm), custom_call_target="tpu_custom_call" | custom-call | tf_op jit(solution)/shard_map/momentum_step/pallas_call | solution.py:523
  39.7 0.6 %copy.7 = f32[1,2,5120]{2,1,0:T(2,128)} copy(f32[1,2,5120]{2,1,0:T(2,128)S(1)} %get-tuple-element.4) | data formatting | bytes 81920
  40.3 0.6 %copy.8 = f32[2,5120]{1,0:T(2,128)} copy(f32[2,5120]{1,0:T(2,128)S(1)} %get-tuple-element.5) | data formatting | bytes 81920
